TPU v7x, 256 devices: a whole 4x4x8 slice. The times are simulated.
256 devices in a mesh: batch: 64 (over x, z, core), proto: 4 (over y).
Axes of the slice: x: 4, y: 4, z: 8, core: 2. Of those that a mesh axis runs over, the one named last changes fastest.
Arguments:
- teacher_tokens: bfloat16 [512, 256, 256], P('batch'), may hold values from -36 to 36
- student_tokens: bfloat16 [512, 256, 256], P('batch'), may hold values from -36 to 36
- masked_index: int32 [512, 64], P('batch'), may hold values from 0 to 255, as said below
- prototypes: bfloat16 [32768, 256], P(('batch', 'proto')), may hold values from -0.375 to 0.375
Outputs:
- loss: float32 [], replicated
- grad_student: bfloat16 [32768, 256], P('batch')
- grad_weight: float32 [32768, 256], P(('batch', 'proto'))
Inputs may be any that keep to these rules, and one draw needn't show every extreme that they name: `masked_index`: each row holds 64 distinct patch positions of its image.
All inputs are finite; a program needn't handle non-finite values.
Results may differ from a plain program's by a relative error of at most 0.0049.
Values may be sent and summed in bfloat16 or wider, within the bound.
No kernel may reach another device: no remote copies, remote signals or barrier semaphores. Data moves between devices by JAX's collectives and lax.ppermute only.
A program may use at most 128 MiB of HBM per device.

v0:
```python
import functools
import math

import jax
import jax.numpy as jnp
from jax import lax
from jax.experimental import pallas as pl
from jax.experimental.pallas import tpu as pltpu
from jax.sharding import Mesh, PartitionSpec as P

X, Z, C, Y = 4, 8, 2, 4
F32, BF16 = jnp.float32, jnp.bfloat16
D = 256
IMAGES = 8
MASKED = 64
OWN_ROWS = 512
OWN_PROTOS = 128
ROWS = X * OWN_ROWS
PROTOS = Z * C * OWN_PROTOS
TOTAL_ROWS = ROWS * Z * C
PEERS = X * Y
LANES = 128
GROUPS = 16
BLOCK = 256
HALVES = BLOCK // LANES
T_SCALE = 1.0 / 0.07
S_SCALE = 1.0 / 0.1
MIB = 1 << 20
UNROLL = 8
LOG2E = math.log2(math.e)
GRAD_SCALE = 1.0 / (0.1 * TOTAL_ROWS)
VMEM_SPEC = pl.BlockSpec(memory_space=pltpu.VMEM)
KERN_BLOCKS = ROWS // BLOCK
TRANS_B = (((1,), (1,)), ((), ()))


def whole(shape):
    return pl.BlockSpec(shape, lambda *_: (0,) * len(shape))


def params(mib=32):
    return pltpu.CompilerParams(vmem_limit_bytes=mib * MIB)


def in_vmem(array):
    return pltpu.with_memory_space_constraint(array, pltpu.VMEM)


def down(row):
    return jnp.transpose(jnp.broadcast_to(row, (LANES, LANES)))


def along(column_parts):
    return jnp.sum(jnp.transpose(column_parts), axis=0, keepdims=True)


def spread(ref, first, at, row):
    ref[:, pl.ds(first + at, 1), :] = jnp.broadcast_to(row[None], (ref.shape[0], 1, LANES))


def pick_kernel(index_ref, tokens_ref, out_ref):
    for image in range(IMAGES):
        at = lax.broadcasted_iota(jnp.int32, (D, MASKED), 0)
        chosen = (at == index_ref[image : image + 1, :]).astype(BF16)
        rows = lax.dot_general(
            chosen, tokens_ref[image], (((0,), (0,)), ((), ())), preferred_element_type=F32
        )
        out_ref[image * MASKED : (image + 1) * MASKED, :] = rows.astype(BF16)


def pick_rows(index, tokens):
    return pl.pallas_call(
        pick_kernel,
        out_shape=jax.ShapeDtypeStruct((OWN_ROWS, D), BF16),
        in_specs=[whole(index.shape), whole(tokens.shape)],
        out_specs=whole((OWN_ROWS, D)),
        grid=(1,),
        compiler_params=params(),
        name="pick_rows",
    )(index, tokens)


def place_rows(pieces, out_ref):
    x = lax.axis_index("x")
    for piece, by in zip(pieces, (0, 2, 1, -1)):
        at = lax.rem(x + X - by, X) * OWN_ROWS
        out_ref[pl.ds(pl.multiple_of(at, OWN_ROWS), OWN_ROWS), :] = piece[...]


def place_protos(pieces, out_ref):
    z, core = lax.axis_index("z"), lax.axis_index("c")
    sign = 1 - 2 * core
    chips = [(z, core)]
    chips += [(lax.rem(z + Z - sign * by, Z), core) for by in (1, 2, 3)]
    chips += [(lax.rem(z + Z + sign * by, Z), 1 - core) for by in (1, 2, 3)]
    far = lax.rem(z + Z // 2, Z)
    chips += [(far, core), (far, 1 - core)]
    for piece, (chip, first) in zip(pieces, chips):
        for half in range(piece.shape[0] // OWN_PROTOS):
            which = first if half == 0 else 1 - first
            at = pl.multiple_of((chip * C + which) * OWN_PROTOS, OWN_PROTOS)
            out_ref[pl.ds(at, OWN_PROTOS), :] = piece[half * OWN_PROTOS : (half + 1) * OWN_PROTOS, :]


def block_rows(block):
    return pl.ds(pl.multiple_of(block * BLOCK, BLOCK), BLOCK)


def in_pairs(multiply, work):
    multiply(0, 0)

    def step(pair, carry):
        for parity in range(2):
            block = 2 * pair + parity
            multiply(jnp.minimum(block + 1, KERN_BLOCKS - 1), 1 - parity)
            work(block, parity)
        return carry

    lax.fori_loop(0, KERN_BLOCKS // 2, step, 0)


def teacher_kernel(*refs):
    rows_in, protos_in = refs[:X], refs[X : X + 9]
    kern_ref, top_ref, tops_ref, protos_ref, rows_ref, *scores_refs = refs[X + 9 :]
    place_rows(rows_in, rows_ref)
    place_protos(protos_in, protos_ref)

    def multiply(block, parity):
        scores_refs[parity][...] = lax.dot_general(
            rows_ref[block_rows(block), :], protos_ref[...], TRANS_B, preferred_element_type=F32
        )

    def work(block, parity):
        scores_ref = scores_refs[parity]
        for half in range(HALVES):
            at = slice(half * LANES, (half + 1) * LANES)
            group_at = block * HALVES + half
            kern_at = pl.ds(pl.multiple_of(group_at * LANES, LANES), LANES)
            top = scores_ref[at, :LANES]
            for group in range(1, GROUPS):
                top = jnp.maximum(top, scores_ref[at, group * LANES : (group + 1) * LANES])
            top = jnp.max(jnp.transpose(top), axis=0, keepdims=True)
            shift = down(top)
            for group in range(GROUPS):
                lanes = slice(group * LANES, (group + 1) * LANES)
                value = jnp.exp2((scores_ref[at, lanes] - shift) * (T_SCALE * LOG2E))
                kern_ref[kern_at, lanes] = value.astype(BF16)
            row = top * T_SCALE
            top_ref[pl.ds(group_at, 1), :] = row
            spread(tops_ref, 0, group_at, row)

    in_pairs(multiply, work)


def teacher_scores(rows, protos):
    return pl.pallas_call(
        teacher_kernel,
        out_shape=(
            pltpu.VMEM((ROWS, PROTOS), BF16),
            jax.ShapeDtypeStruct((GROUPS, LANES), F32),
            jax.ShapeDtypeStruct((PEERS, GROUPS, LANES), F32),
            jax.ShapeDtypeStruct((PROTOS, D), BF16),
        ),
        in_specs=[VMEM_SPEC] * (X + 9),
        out_specs=(VMEM_SPEC,) * 4,
        scratch_shapes=[pltpu.VMEM((ROWS, D), BF16)] + [pltpu.VMEM((BLOCK, PROTOS), F32)] * 2,
        compiler_params=params(),
        name="teacher_scores",
    )(*rows, *protos)


def weight_kernel(top_ref, got_ref, out_ref):
    got = got_ref[0]
    for peer in range(1, PEERS):
        got = jnp.maximum(got, got_ref[peer])
    out_ref[...] = jnp.exp(top_ref[...] - got)


def row_weight(top, got):
    return pl.pallas_call(
        weight_kernel,
        out_shape=jax.ShapeDtypeStruct((GROUPS, LANES), F32),
        in_specs=[VMEM_SPEC] * 2,
        out_specs=VMEM_SPEC,
        compiler_params=params(),
        name="row_weight",
    )(top, got)


def column_kernel(first, weight_ref, *refs):
    if first:
        kern_ref, sums_ref, acc_ref = refs
        scaled_ref = weight_ref
    else:
        got_ref, kern_ref, sums_ref, acc_ref, scaled_ref = refs
        scaled_ref[...] = weight_ref[...] / jnp.sum(got_ref[...], axis=0)
    acc_ref[...] = jnp.zeros_like(acc_ref)

    def step(block, carry):
        rows = pl.ds(pl.multiple_of(block * LANES, LANES), LANES)
        weight = down(scaled_ref[pl.ds(block, 1), :])
        for group in range(GROUPS):
            part = kern_ref[rows, group * LANES : (group + 1) * LANES].astype(F32) * weight
            acc_ref[group] += jnp.sum(part.reshape(LANES // 8, 8, LANES), axis=0)
        return carry

    lax.fori_loop(0, GROUPS, step, 0, unroll=UNROLL)
    for group in range(GROUPS):
        spread(sums_ref, 0, group, jnp.sum(acc_ref[group], axis=0, keepdims=True))


def column_pass(weight, kern, got=None):
    first = got is None
    scratch = [pltpu.VMEM((GROUPS, 8, LANES), F32)] + ([] if first else [pltpu.VMEM((GROUPS, LANES), F32)])
    inputs = (weight,) if first else (weight, got)
    return pl.pallas_call(
        functools.partial(column_kernel, first),
        out_shape=jax.ShapeDtypeStruct((Z * C, GROUPS, LANES), F32),
        in_specs=[VMEM_SPEC] * (len(inputs) + 1),
        out_specs=VMEM_SPEC,
        scratch_shapes=scratch,
        compiler_params=params(),
        name="column_pass",
    )(*inputs, in_vmem(kern))


def row_kernel(weight_ref, got_ref, kern_ref, sums_ref, scale_ref):
    scale_ref[...] = 1.0 / jnp.sum(got_ref[...], axis=0)

    def step(block, carry):
        rows = pl.ds(pl.multiple_of(block * LANES, LANES), LANES)
        weight = down(weight_ref[pl.ds(block, 1), :])
        total = jnp.zeros((LANES, LANES), F32)
        for group in range(GROUPS):
            part = kern_ref[rows, group * LANES : (group + 1) * LANES].astype(F32) * weight
            total += part * scale_ref[group : group + 1, :]
        spread(sums_ref, 0, block, along(total))
        return carry

    lax.fori_loop(0, GROUPS, step, 0, unroll=UNROLL)


def row_pass(weight, got, kern):
    return pl.pallas_call(
        row_kernel,
        out_shape=(
            jax.ShapeDtypeStruct((PEERS, GROUPS, LANES), F32),
            jax.ShapeDtypeStruct((GROUPS, LANES), F32),
        ),
        in_specs=[VMEM_SPEC] * 3,
        out_specs=(VMEM_SPEC, VMEM_SPEC),
        compiler_params=params(),
        name="row_pass",
    )(weight, got, in_vmem(kern))


def last_kernel(weight_ref, got_ref, protos_ref, *refs):
    rows_in, (kern_ref, sums_ref, scale_ref, rows_ref, *scores_refs) = refs[:X], refs[X:]
    place_rows(rows_in, rows_ref)
    scale_ref[...] = 1.0 / jnp.sum(got_ref[...], axis=0)

    def multiply(block, parity):
        scores_refs[parity][...] = lax.dot_general(
            rows_ref[block_rows(block), :], protos_ref[...], TRANS_B, preferred_element_type=F32
        )

    def work(block, parity):
        scores_ref = scores_refs[parity]
        for half in range(HALVES):
            group_at = block * HALVES + half
            weight = down(weight_ref[pl.ds(group_at, 1), :])
            total = jnp.zeros((LANES, LANES), F32)
            crossed = jnp.zeros((LANES, LANES), F32)
            top = jnp.full((LANES, LANES), -jnp.inf, F32)
            at = slice(half * LANES, (half + 1) * LANES)
            kern_at = pl.ds(pl.multiple_of(group_at * LANES, LANES), LANES)
            for group in range(GROUPS):
                lanes = slice(group * LANES, (group + 1) * LANES)
                part = (kern_ref[kern_at, lanes].astype(F32) * weight) * scale_ref[group : group + 1, :]
                total += part
                scores = scores_ref[at, lanes]
                crossed += part * scores
                top = jnp.maximum(top, scores)
            top = jnp.max(jnp.transpose(top), axis=0, keepdims=True) * (S_SCALE * LOG2E)
            shift = down(top)
            spent = jnp.zeros((LANES, LANES), F32)
            for group in range(GROUPS):
                lanes = slice(group * LANES, (group + 1) * LANES)
                spent += jnp.exp2(scores_ref[at, lanes] * (S_SCALE * LOG2E) - shift)
            spread(sums_ref, 0, group_at, along(total))
            spread(sums_ref, GROUPS, group_at, along(crossed) * S_SCALE)
            spread(sums_ref, 2 * GROUPS, group_at, jnp.log2(along(spent)) + top)

    in_pairs(multiply, work)


def last_pass(weight, got, protos, rows, kern):
    return pl.pallas_call(
        last_kernel,
        out_shape=(
            jax.ShapeDtypeStruct((PEERS, 3 * GROUPS, LANES), F32),
            jax.ShapeDtypeStruct((GROUPS, LANES), F32),
            jax.ShapeDtypeStruct((ROWS, D), BF16),
        ),
        in_specs=[VMEM_SPEC] * (X + 4),
        out_specs=(VMEM_SPEC,) * 3,
        scratch_shapes=[pltpu.VMEM((BLOCK, PROTOS), F32)] * 2,
        compiler_params=params(),
        name="last_pass",
    )(weight, got, protos, *rows, in_vmem(kern))


def grad_kernel(
    weight_ref, got_ref, scale_ref, kern_ref, rows_ref, protos_ref, student_ref, keep_ref, send_ref, loss_ref,
    scaled_ref, lse_ref, acc_ref, *scratch,
):
    scores_refs, logits_refs = scratch[:2], scratch[2:]
    sums = jnp.sum(got_ref[:, :GROUPS, :], axis=0)
    crossed = jnp.sum(got_ref[:, GROUPS : 2 * GROUPS, :], axis=0)
    top = got_ref[0, 2 * GROUPS :, :]
    for peer in range(1, PEERS):
        top = jnp.maximum(top, got_ref[peer, 2 * GROUPS :, :])
    total = jnp.zeros_like(top)
    for peer in range(PEERS):
        total += jnp.exp2(got_ref[peer, 2 * GROUPS :, :] - top)
    lse = top + jnp.log2(total)
    lse_ref[...] = lse - math.log2(GRAD_SCALE)
    scaled_ref[...] = weight_ref[...] / sums * GRAD_SCALE
    terms = (lse * math.log(2.0) * sums - crossed) / sums
    terms = jnp.sum(jnp.sum(terms, axis=0, keepdims=True), axis=1, keepdims=True)
    loss_ref[...] = jnp.broadcast_to(terms, (8, LANES))

    logits_refs[1][...] = jnp.zeros((BLOCK, PROTOS), BF16)
    acc_ref[...] = jnp.zeros_like(acc_ref)

    def multiply(block, parity):
        scores_refs[parity][...] = lax.dot_general(
            rows_ref[block_rows(block), :], protos_ref[...], TRANS_B, preferred_element_type=F32
        )

    def reduce(block, parity):
        logits = logits_refs[parity][...]
        student_ref[block_rows(block), :] = jnp.dot(
            logits, protos_ref[...], preferred_element_type=F32
        ).astype(BF16)
        acc_ref[...] += jnp.dot(
            jnp.transpose(rows_ref[block_rows(block), :]), logits, preferred_element_type=F32
        )

    def work(block, parity):
        reduce(jnp.maximum(block - 1, 0), 1 - parity)
        for half in range(HALVES):
            group_at = block * HALVES + half
            weight = down(scaled_ref[pl.ds(group_at, 1), :])
            lse = down(lse_ref[pl.ds(group_at, 1), :])
            kern_at = pl.ds(pl.multiple_of(group_at * LANES, LANES), LANES)
            for group in range(GROUPS):
                lanes = slice(group * LANES, (group + 1) * LANES)
                at = (slice(half * LANES, (half + 1) * LANES), lanes)
                target = (kern_ref[kern_at, lanes].astype(F32) * weight) * scale_ref[group : group + 1, :]
                prob = jnp.exp2(scores_refs[parity][at] * (S_SCALE * LOG2E) - lse)
                logits_refs[parity][at] = (prob - target).astype(BF16)

    in_pairs(multiply, work)
    reduce(KERN_BLOCKS - 1, 1)

    core = lax.axis_index("c")
    for z in range(Z):
        for c in range(C):
            first = (z * C + c) * OWN_PROTOS
            part = jnp.transpose(acc_ref[:, first : first + OWN_PROTOS])

            @pl.when(core == c)
            def _(part=part, z=z):
                keep_ref[z] = part

            @pl.when(core != c)
            def _(part=part, z=z):
                send_ref[z] = part.astype(BF16)


def gradients(weight, got, scale, kern, rows, protos):
    return pl.pallas_call(
        grad_kernel,
        out_shape=(
            pltpu.HBM((ROWS, D), BF16),
            jax.ShapeDtypeStruct((Z, OWN_PROTOS, D), F32),
            jax.ShapeDtypeStruct((Z, OWN_PROTOS, D), BF16),
            jax.ShapeDtypeStruct((8, LANES), F32),
        ),
        in_specs=[VMEM_SPEC] * 6,
        out_specs=(VMEM_SPEC,) * 4,
        scratch_shapes=[
            pltpu.VMEM((GROUPS, LANES), F32),
            pltpu.VMEM((GROUPS, LANES), F32),
            pltpu.VMEM((D, PROTOS), F32),
        ]
        + [pltpu.VMEM((BLOCK, PROTOS), F32)] * 2
        + [pltpu.VMEM((BLOCK, PROTOS), BF16)] * 2,
        compiler_params=params(),
        name="gradients",
    )(weight, got, scale, in_vmem(kern), rows, protos)


TAIL = 16


def split_kernel(keep_ref, got_ref, loss_ref, other_ref, mine_ref, *outs):
    value = jnp.broadcast_to((loss_ref[...] + other_ref[...])[0:1, :], (TAIL, LANES))
    high = value.astype(BF16)
    rest = value - high.astype(F32)
    middle = rest.astype(BF16)
    low = (rest - middle.astype(F32)).astype(BF16)
    row = lax.broadcasted_iota(jnp.int32, (TAIL, LANES), 0)
    tail = jnp.where(row == 0, high.astype(F32), jnp.where(row == 1, middle.astype(F32), low.astype(F32)))
    tail = jnp.concatenate([tail, tail], axis=1).astype(BF16)
    for shift, out in enumerate(outs):
        at = lax.rem(lax.axis_index("z") + shift, Z)
        part = keep_ref[at] + got_ref[at].astype(F32)
        if shift == 0:
            mine_ref[...] = part
        out[:OWN_PROTOS, :] = part.astype(BF16)
        out[OWN_PROTOS:, :] = tail


def split_sums(keep, got, loss, other):
    return pl.pallas_call(
        split_kernel,
        out_shape=(jax.ShapeDtypeStruct((OWN_PROTOS, D), F32),)
        + (jax.ShapeDtypeStruct((OWN_PROTOS + TAIL, D), BF16),) * Z,
        in_specs=[VMEM_SPEC] * 4,
        out_specs=(VMEM_SPEC,) * (Z + 1),
        compiler_params=params(),
        name="split_sums",
    )(keep, got, loss, other)


def join_kernel(mine_ref, *refs):
    parts, (out_ref, loss_ref, value_ref) = refs[:Z], refs[Z:]
    total = mine_ref[...]
    for shift, part in enumerate(parts):
        if shift:
            total += part[:OWN_PROTOS, :].astype(F32)
        tail = part[OWN_PROTOS:, :LANES].astype(F32)
        at = lax.rem(lax.axis_index("z") + Z - shift, Z)
        value_ref[pl.ds(at, 1), :] = tail[0:1] + (tail[1:2] + tail[2:3])
    out_ref[...] = total
    loss = value_ref[0:1, :]
    for z in range(1, Z):
        loss = loss + value_ref[z : z + 1, :]
    loss_ref[...] = jnp.broadcast_to(loss, (8, LANES)) * (1.0 / TOTAL_ROWS)


def join_sums(mine, parts):
    return pl.pallas_call(
        join_kernel,
        out_shape=(jax.ShapeDtypeStruct((OWN_PROTOS, D), F32), jax.ShapeDtypeStruct((8, LANES), F32)),
        in_specs=[VMEM_SPEC] * (Z + 1),
        out_specs=(VMEM_SPEC, VMEM_SPEC),
        scratch_shapes=[pltpu.VMEM((Z, LANES), F32)],
        compiler_params=params(),
        name="join_sums",
    )(mine, *parts)


def shift_x(value, by):
    return lax.ppermute(value, "x", [(i, (i + by) % X) for i in range(X)])


def shift_z(value, by):
    return lax.ppermute(value, "z", [(i, (i + by) % Z) for i in range(Z)])


def swap_core(value):
    return lax.ppermute(value, "c", [(0, 1), (1, 0)])


def fan_z(value, by):
    pairs = [(z * C + c, (z + (by if c == 0 else -by)) % Z * C + c) for z in range(Z) for c in range(C)]
    return lax.ppermute(value, ("z", "c"), pairs)


def over_rows(parts):
    return lax.all_to_all(parts, ("x", "y"), 0, 0, tiled=True)


def over_protos(parts):
    return lax.all_to_all(parts, ("z", "c"), 0, 0, tiled=True)


def over_y(parts):
    return lax.all_to_all(parts, "y", 0, 0, tiled=True)


def body(teacher_tokens, student_tokens, masked_index, prototypes):
    teacher_rows = pick_rows(masked_index, teacher_tokens)
    teacher_rows, prototypes = lax.optimization_barrier((teacher_rows, prototypes))
    other = swap_core(prototypes)
    far_own = shift_z(prototypes, Z // 2)
    teacher_in = [teacher_rows] + [shift_x(teacher_rows, by) for by in (2, 1, -1)]
    chip_protos = jnp.concatenate([prototypes, other], axis=0)
    near = [fan_z(chip_protos, by) for by in (1, 2, 3)]
    far_own, near[2], student_tokens = lax.optimization_barrier((far_own, near[2], student_tokens))
    student_rows = pick_rows(masked_index, student_tokens)
    student_in = [student_rows] + [shift_x(student_rows, by) for by in (2, 1, -1)]
    protos_in = [chip_protos, *near, *[swap_core(part) for part in near], far_own, swap_core(far_own)]

    kern, top, tops, protos = teacher_scores(teacher_in, protos_in)
    weight = row_weight(top, over_rows(tops))
    weight, student_in = lax.optimization_barrier((weight, student_in))
    sums = column_pass(weight, kern)
    got, _ = row_pass(weight, over_protos(sums), kern)
    sums = column_pass(weight, kern, over_rows(got))
    got, _ = row_pass(weight, over_protos(sums), kern)
    sums = column_pass(weight, kern, over_rows(got))
    got, scale, rows = last_pass(weight, over_protos(sums), protos, student_in, kern)
    student, keep, send, loss = gradients(weight, over_rows(got), scale, kern, rows, protos)

    mine, own, *sends = split_sums(keep, swap_core(send), loss, swap_core(loss))
    parts = [own] + [None] * (Z - 1)
    for by in (4, 3, 5, 2, 6, 1, 7):
        parts[by] = shift_z(sends[by - 1], by)
    student = over_rows(student.reshape(PEERS, ROWS // PEERS, D))
    student, parts[2:6] = lax.optimization_barrier((student, parts[2:6]))
    student = jnp.sum(student.astype(F32), axis=0).astype(BF16)
    student = over_y(jnp.broadcast_to(student[None], (Y,) + student.shape))
    grad_weight, loss = join_sums(mine, parts)
    return loss[0, 0], student.reshape(OWN_ROWS, D), grad_weight


def solution(mesh):
    named = Mesh(mesh.devices.reshape(X, Z, C, Y), ("x", "z", "c", "y"))
    batch = ("x", "z", "c")
    placed = (
        P(batch, None, None),
        P(batch, None, None),
        P(batch, None),
        P((*batch, "y"), None),
    )
    return jax.shard_map(
        body,
        mesh=named,
        in_specs=placed,
        out_specs=(P(), P(batch, None), P((*batch, "y"), None)),
        check_vma=False,
    )
```

profile of v0, /device:TPU:8, one launch (start us, length us, event | category | flops | bytes accessed | tf_op | source)
XLA Modules:
  0.0 199.8 jit_solution(4610044208011079456)
XLA Ops:
  4.5 4.6 %collective-permute-start.7 = (bf16[256,256]{1,0:T(8,128)(2,1)S(1)}, bf16[256,256]{1,0:T(8,128)(2,1)S(1)}, u32[]{:S(2)}, u32[]{:S(2)}) collective-permute-start(bf16[256,256]{1,0:T(8,128)(2,1)S(1)} %constant_dynamic-update-slice_fusion.refs_4_), channel_id=1, source_target_pairs={{0,24},{4,44},{8,32},{12,52},{16,40},{20,60},{24,48},{28,4},{32,56... | collective-permute-start | bytes 393224 | tf_op jit(solution)/shard_map/ppermute | solution.py:480
  9.1 4.5 %collective-permute-start.6 = (bf16[128,256]{1,0:T(8,128)(2,1)}, bf16[128,256]{1,0:T(8,128)(2,1)S(1)}, u32[]{:S(2)}, u32[]{:S(2)}) collective-permute-start(bf16[128,256]{1,0:T(8,128)(2,1)} %param.7), channel_id=1, source_target_pairs={{0,32},{8,40},{16,48},{24,56},{32,0},{40,8},{48,16},{56,24},{1,33}... | collective-permute-start | bytes 196616 | tf_op jit(solution)/shard_map/ppermute | solution.py:471
  13.6 2.8 %collective-permute-start.2 = (bf16[512,256]{1,0:T(8,128)(2,1)S(1)}, bf16[512,256]{1,0:T(8,128)(2,1)S(1)}, u32[]{:S(2)}, u32[]{:S(2)}) collective-permute-start(bf16[512,256]{1,0:T(8,128)(2,1)S(1)} %pick_rows.2.refs_0_), channel_id=1, source_target_pairs={{0,192},{64,0},{128,64},{192,128},{1,193},{65,1},{129,65},{193,129... | collective-permute-start | bytes 786440 | tf_op jit(solution)/shard_map/ppermute | solution.py:467
  16.3 3.3 %collective-permute-done.6.refs_11_ = bf16[128,256]{1,0:T(8,128)(2,1)S(1)} collective-permute-done((bf16[128,256]{1,0:T(8,128)(2,1)}, bf16[128,256]{1,0:T(8,128)(2,1)S(1)}, u32[]{:S(2)}, u32[]{:S(2)}) %collective-permute-start.6) | collective-permute-done | bytes 65568 | tf_op jit(solution)/shard_map/ppermute | solution.py:471
  19.6 3.0 %collective-permute-start = (bf16[512,256]{1,0:T(8,128)(2,1)S(1)}, bf16[512,256]{1,0:T(8,128)(2,1)S(1)}, u32[]{:S(2)}, u32[]{:S(2)}) collective-permute-start(bf16[512,256]{1,0:T(8,128)(2,1)S(1)} %pick_rows.2.refs_0_), channel_id=1, source_target_pairs={{0,128},{64,192},{128,0},{192,64},{1,129},{65,193},{129,1},{193,65... | collective-permute-start | bytes 786440 | tf_op jit(solution)/shard_map/ppermute | solution.py:467
  23.7 5.1 %collective-permute-done.4.refs_5_ = bf16[256,256]{1,0:T(8,128)(2,1)S(1)} collective-permute-done((bf16[256,256]{1,0:T(8,128)(2,1)S(1)}, bf16[256,256]{1,0:T(8,128)(2,1)S(1)}, u32[]{:S(2)}, u32[]{:S(2)}) %collective-permute-start.4) | collective-permute-done | bytes 131104 | tf_op jit(solution)/shard_map/ppermute | solution.py:480
  34.8 6.4 %teacher_scores.1 = (bf16[2048,2048]{1,0:T(8,128)(2,1)S(1)}, f32[16,128]{1,0:T(8,128)S(1)}, f32[16,16,128]{2,1,0:T(8,128)S(1)}, bf16[2048,256]{1,0:T(8,128)(2,1)S(1)}) custom-call(bf16[512,256]{1,0:T(8,128)(2,1)S(1)} %pick_rows.2.refs_0_, bf16[512,256]{1,0:T(8,128)(2,1)S(1)} %collective-permute-done.refs_1_, ...), custom_call_target="tpu_custom_call" | custom-call | tf_op jit(solution)/shard_map/teacher_scores/pallas_call | solution.py:156
  41.1 13.6 %all_to_all.45.got_ref = f32[16,16,128]{2,1,0:T(8,128)S(1)} all-to-all(f32[16,16,128]{2,1,0:T(8,128)S(1)} %get-tuple-element.47), channel_id=1, replica_groups=mesh['x'=4,'z'=8,'c'=2,'y'=4] {'x','y'}, dimensions={0} | all-to-all | bytes 262144 | tf_op jit(solution)/shard_map/all_to_all | solution.py:484
  54.8 1.8 column_pass.3
  56.6 13.3 %all_to_all.46.got_ref = f32[16,16,128]{2,1,0:T(8,128)S(1)} all-to-all(f32[16,16,128]{2,1,0:T(8,128)S(1)} %column_pass.3), channel_id=1, replica_groups=mesh['x'=4,'z'=8,'c'=2,'y'=4] {'z','c'}, dimensions={0} | all-to-all | bytes 262144 | tf_op jit(solution)/shard_map/all_to_all | solution.py:488
  69.9 2.5 %row_pass.2 = (f32[16,16,128]{2,1,0:T(8,128)S(1)}, f32[16,128]{1,0:T(8,128)}) custom-call(f32[16,128]{1,0:T(8,128)S(1)} %row_weight.1.weight_ref, f32[16,16,128]{2,1,0:T(8,128)S(1)} %all_to_all.46.got_ref, bf16[2048,2048]{1,0:T(8,128)(2,1)S(1)} %get-tuple-element.50.refs_0_.kern_ref.refs_1_.refs_4_), custom_call_target="tpu_custom_call" | custom-call | tf_op jit(solution)/shard_map/row_pass/pallas_call | solution.py:244
  72.3 11.6 %all_to_all.47.refs_0_ = f32[16,16,128]{2,1,0:T(8,128)S(1)} all-to-all(f32[16,16,128]{2,1,0:T(8,128)S(1)} %get-tuple-element.51), channel_id=1, replica_groups=mesh['x'=4,'z'=8,'c'=2,'y'=4] {'x','y'}, dimensions={0} | all-to-all | bytes 262144 | tf_op jit(solution)/shard_map/all_to_all | solution.py:484
  84.0 1.9 column_pass.4
  85.8 11.3 %all_to_all.48.got_ref = f32[16,16,128]{2,1,0:T(8,128)S(1)} all-to-all(f32[16,16,128]{2,1,0:T(8,128)S(1)} %column_pass.4), channel_id=1, replica_groups=mesh['x'=4,'z'=8,'c'=2,'y'=4] {'z','c'}, dimensions={0} | all-to-all | bytes 262144 | tf_op jit(solution)/shard_map/all_to_all | solution.py:488
  97.2 2.5 %row_pass.3 = (f32[16,16,128]{2,1,0:T(8,128)S(1)}, f32[16,128]{1,0:T(8,128)}) custom-call(f32[16,128]{1,0:T(8,128)S(1)} %row_weight.1.weight_ref, f32[16,16,128]{2,1,0:T(8,128)S(1)} %all_to_all.48.got_ref, bf16[2048,2048]{1,0:T(8,128)(2,1)S(1)} %get-tuple-element.50.refs_0_.kern_ref.refs_1_.refs_4_), custom_call_target="tpu_custom_call" | custom-call | tf_op jit(solution)/shard_map/row_pass/pallas_call | solution.py:244
  99.6 11.5 %all_to_all.49.refs_0_ = f32[16,16,128]{2,1,0:T(8,128)S(1)} all-to-all(f32[16,16,128]{2,1,0:T(8,128)S(1)} %get-tuple-element.52), channel_id=1, replica_groups=mesh['x'=4,'z'=8,'c'=2,'y'=4] {'x','y'}, dimensions={0} | all-to-all | bytes 262144 | tf_op jit(solution)/shard_map/all_to_all | solution.py:484
  111.1 1.9 column_pass.5
  113.0 11.3 %all_to_all.50.got_ref = f32[16,16,128]{2,1,0:T(8,128)S(1)} all-to-all(f32[16,16,128]{2,1,0:T(8,128)S(1)} %column_pass.5), channel_id=1, replica_groups=mesh['x'=4,'z'=8,'c'=2,'y'=4] {'z','c'}, dimensions={0} | all-to-all | bytes 262144 | tf_op jit(solution)/shard_map/all_to_all | solution.py:488
  124.3 8.8 %last_pass.1 = (f32[16,48,128]{2,1,0:T(8,128)S(1)}, f32[16,128]{1,0:T(8,128)S(1)}, bf16[2048,256]{1,0:T(8,128)(2,1)S(1)}) custom-call(f32[16,128]{1,0:T(8,128)S(1)} %row_weight.1.weight_ref, f32[16,16,128]{2,1,0:T(8,128)S(1)} %all_to_all.50.got_ref, bf16[2048,256]{1,0:T(8,128)(2,1)S(1)} %get-tuple-element.53.protos_ref, ...), custom_call_target="tpu_custom_call" | custom-call | tf_op jit(solution)/shard_map/last_pass/pallas_call | solution.py:298
  133.2 14.4 %all_to_all.51.got_ref = f32[16,48,128]{2,1,0:T(8,128)S(1)} all-to-all(f32[16,48,128]{2,1,0:T(8,128)S(1)} %get-tuple-element.58), channel_id=1, replica_groups=mesh['x'=4,'z'=8,'c'=2,'y'=4] {'x','y'}, dimensions={0} | all-to-all | bytes 786432 | tf_op jit(solution)/shard_map/all_to_all | solution.py:484
  147.5 13.5 %gradients.1 = (bf16[2048,256]{1,0:T(8,128)(2,1)}, f32[8,128,256]{2,1,0:T(8,128)S(1)}, bf16[8,128,256]{2,1,0:T(8,128)(2,1)S(1)}, f32[8,128]{1,0:T(8,128)S(1)}) custom-call(f32[16,128]{1,0:T(8,128)S(1)} %row_weight.1.weight_ref, f32[16,48,128]{2,1,0:T(8,128)S(1)} %all_to_all.51.got_ref, f32[16,128]{1,0:T(8,128)S(1)} %get-tuple-element.59.scale_ref, ...), custom_call_target="tpu_custom_call" | custom-call | tf_op jit(solution)/shard_map/gradients/pallas_call | solution.py:383
  161.0 4.9 %all-to-all-start.7 = ((bf16[16,128,256]{2,1,0:T(8,128)(2,1)}), bf16[16,128,256]{2,1,0:T(8,128)(2,1)S(1)}, u32[]{:S(2)}, u32[]{:S(2)}) async-start(bf16[16,128,256]{2,1,0:T(8,128)(2,1)} %bitcast.3), calls=%async_computation.7 | async-start | bytes 2097152 | tf_op jit(solution)/shard_map/all_to_all | solution.py:484
  166.4 1.4 collective-permute-done.16.other_ref
  168.5 1.3 collective-permute-start.19
  169.9 4.4 %collective-permute-start.20 = (bf16[144,256]{1,0:T(8,128)(2,1)S(1)}, bf16[144,256]{1,0:T(8,128)(2,1)S(1)}, u32[]{:S(2)}, u32[]{:S(2)}) collective-permute-start(bf16[144,256]{1,0:T(8,128)(2,1)S(1)} %get-tuple-element.70), channel_id=1, source_target_pairs={{0,32},{8,40},{16,48},{24,56},{32,0},{40,8},{48,16},{56,24},{1,33}... | collective-permute-start | bytes 221192 | tf_op jit(solution)/shard_map/ppermute | solution.py:471
  174.2 1.8 collective-permute-start.21
  176.0 3.0 %collective-permute-done.18.refs_2_ = bf16[144,256]{1,0:T(8,128)(2,1)S(1)} collective-permute-done((bf16[144,256]{1,0:T(8,128)(2,1)S(1)}, bf16[144,256]{1,0:T(8,128)(2,1)S(1)}, u32[]{:S(2)}, u32[]{:S(2)}) %collective-permute-start.18) | collective-permute-done | bytes 73760 | tf_op jit(solution)/shard_map/ppermute | solution.py:471
  179.0 3.1 %collective-permute-done.20.refs_4_ = bf16[144,256]{1,0:T(8,128)(2,1)S(1)} collective-permute-done((bf16[144,256]{1,0:T(8,128)(2,1)S(1)}, bf16[144,256]{1,0:T(8,128)(2,1)S(1)}, u32[]{:S(2)}, u32[]{:S(2)}) %collective-permute-start.20) | collective-permute-done | bytes 73760 | tf_op jit(solution)/shard_map/ppermute | solution.py:471
  183.9 4.8 %all-to-all-start.8 = ((bf16[4,128,256]{2,1,0:T(8,128)(2,1)}), bf16[4,128,256]{2,1,0:T(8,128)(2,1)S(1)}, u32[]{:S(2)}, u32[]{:S(2)}) async-start(bf16[4,128,256]{2,1,0:T(8,128)(2,1)} %broadcast_in_dim.2), calls=%async_computation.8 | async-start | bytes 524288 | tf_op jit(solution)/shard_map/all_to_all | solution.py:492
  188.8 2.9 %collective-permute-start.17 = (bf16[144,256]{1,0:T(8,128)(2,1)S(1)}, bf16[144,256]{1,0:T(8,128)(2,1)S(1)}, u32[]{:S(2)}, u32[]{:S(2)}) collective-permute-start(bf16[144,256]{1,0:T(8,128)(2,1)S(1)} %get-tuple-element.66), channel_id=1, source_target_pairs={{0,8},{8,16},{16,24},{24,32},{32,40},{40,48},{48,56},{56,0},{1,9},... | collective-permute-start | bytes 221192 | tf_op jit(solution)/shard_map/ppermute | solution.py:471
  192.5 1.8 collective-permute-start.23
  194.4 3.5 %collective-permute-done.22.refs_6_ = bf16[144,256]{1,0:T(8,128)(2,1)S(1)} collective-permute-done((bf16[144,256]{1,0:T(8,128)(2,1)S(1)}, bf16[144,256]{1,0:T(8,128)(2,1)S(1)}, u32[]{:S(2)}, u32[]{:S(2)}) %collective-permute-start.22) | collective-permute-done | bytes 73760 | tf_op jit(solution)/shard_map/ppermute | solution.py:471
  (52 shorter events, 16.7 us)
Async XLA Ops:
  0.6 1.2 copy-start
  1.9 0.7 copy-start.2
  2.9 1.6 collective-permute-start.3
  4.5 18.2 %collective-permute-start.7 = (bf16[256,256]{1,0:T(8,128)(2,1)S(1)}, bf16[256,256]{1,0:T(8,128)(2,1)S(1)}, u32[]{:S(2)}, u32[]{:S(2)}) collective-permute-start(bf16[256,256]{1,0:T(8,128)(2,1)S(1)} %constant_dynamic-update-slice_fusion.refs_4_), channel_id=1, source_target_pairs={{0,24},{4,44},{8,32},{12,52},{16,40},{20,60},{24,48},{28,4},{32,56... | collective-permute-start | bytes 393224 | tf_op jit(solution)/shard_map/ppermute | solution.py:480
  9.1 10.5 %collective-permute-start.6 = (bf16[128,256]{1,0:T(8,128)(2,1)}, bf16[128,256]{1,0:T(8,128)(2,1)S(1)}, u32[]{:S(2)}, u32[]{:S(2)}) collective-permute-start(bf16[128,256]{1,0:T(8,128)(2,1)} %param.7), channel_id=1, source_target_pairs={{0,32},{8,40},{16,48},{24,56},{32,0},{40,8},{48,16},{56,24},{1,33}... | collective-permute-start | bytes 196616 | tf_op jit(solution)/shard_map/ppermute | solution.py:471
  13.6 18.1 %collective-permute-start.2 = (bf16[512,256]{1,0:T(8,128)(2,1)S(1)}, bf16[512,256]{1,0:T(8,128)(2,1)S(1)}, u32[]{:S(2)}, u32[]{:S(2)}) collective-permute-start(bf16[512,256]{1,0:T(8,128)(2,1)S(1)} %pick_rows.2.refs_0_), channel_id=1, source_target_pairs={{0,192},{64,0},{128,64},{192,128},{1,193},{65,1},{129,65},{193,129... | collective-permute-start | bytes 786440 | tf_op jit(solution)/shard_map/ppermute | solution.py:467
  16.3 16.2 %collective-permute-start.1 = (bf16[512,256]{1,0:T(8,128)(2,1)S(1)}, bf16[512,256]{1,0:T(8,128)(2,1)S(1)}, u32[]{:S(2)}, u32[]{:S(2)}) collective-permute-start(bf16[512,256]{1,0:T(8,128)(2,1)S(1)} %pick_rows.2.refs_0_), channel_id=1, source_target_pairs={{0,64},{64,128},{128,192},{192,0},{1,65},{65,129},{129,193},{193,1... | collective-permute-start | bytes 786440 | tf_op jit(solution)/shard_map/ppermute | solution.py:467
  16.3 7.4 %collective-permute-start.5 = (bf16[256,256]{1,0:T(8,128)(2,1)S(1)}, bf16[256,256]{1,0:T(8,128)(2,1)S(1)}, u32[]{:S(2)}, u32[]{:S(2)}) collective-permute-start(bf16[256,256]{1,0:T(8,128)(2,1)S(1)} %constant_dynamic-update-slice_fusion.refs_4_), channel_id=1, source_target_pairs={{0,16},{4,52},{8,24},{12,60},{16,32},{20,4},{24,40},{28,12},{32,48... | collective-permute-start | bytes 393224 | tf_op jit(solution)/shard_map/ppermute | solution.py:480
  19.6 13.6 %collective-permute-start = (bf16[512,256]{1,0:T(8,128)(2,1)S(1)}, bf16[512,256]{1,0:T(8,128)(2,1)S(1)}, u32[]{:S(2)}, u32[]{:S(2)}) collective-permute-start(bf16[512,256]{1,0:T(8,128)(2,1)S(1)} %pick_rows.2.refs_0_), channel_id=1, source_target_pairs={{0,128},{64,192},{128,0},{192,64},{1,129},{65,193},{129,1},{193,65... | collective-permute-start | bytes 786440 | tf_op jit(solution)/shard_map/ppermute | solution.py:467
  22.6 6.2 %collective-permute-start.4 = (bf16[256,256]{1,0:T(8,128)(2,1)S(1)}, bf16[256,256]{1,0:T(8,128)(2,1)S(1)}, u32[]{:S(2)}, u32[]{:S(2)}) collective-permute-start(bf16[256,256]{1,0:T(8,128)(2,1)S(1)} %constant_dynamic-update-slice_fusion.refs_4_), channel_id=1, source_target_pairs={{0,8},{4,60},{8,16},{12,4},{16,24},{20,12},{24,32},{28,20},{32,40}... | collective-permute-start | bytes 393224 | tf_op jit(solution)/shard_map/ppermute | solution.py:480
  23.7 9.5 %collective-permute-start.10 = (bf16[256,256]{1,0:T(8,128)(2,1)S(1)}, bf16[256,256]{1,0:T(8,128)(2,1)S(1)}, u32[]{:S(2)}, u32[]{:S(2)}) collective-permute-start(bf16[256,256]{1,0:T(8,128)(2,1)S(1)} %collective-permute-done.7.refs_7_), channel_id=1, source_target_pairs={{0,4},{4,0},{1,5},{5,1},{2,6},{6,2},{3,7},{7,3},{8,12},{12,8},{9,1... | collective-permute-start | bytes 393224 | tf_op jit(solution)/shard_map/ppermute | solution.py:475
  28.8 1.6 collective-permute-start.11
  28.8 1.2 copy-start.1
  30.4 24.3 %collective-permute-start.14 = (bf16[512,256]{1,0:T(8,128)(2,1)S(1)}, bf16[512,256]{1,0:T(8,128)(2,1)S(1)}, u32[]{:S(2)}, u32[]{:S(2)}) collective-permute-start(bf16[512,256]{1,0:T(8,128)(2,1)S(1)} %pick_rows.3.refs_0_), channel_id=1, source_target_pairs={{0,192},{64,0},{128,64},{192,128},{1,193},{65,1},{129,65},{193,129... | collective-permute-start | bytes 786440 | tf_op jit(solution)/shard_map/ppermute | solution.py:467
  31.6 23.1 %collective-permute-start.13 = (bf16[512,256]{1,0:T(8,128)(2,1)S(1)}, bf16[512,256]{1,0:T(8,128)(2,1)S(1)}, u32[]{:S(2)}, u32[]{:S(2)}) collective-permute-start(bf16[512,256]{1,0:T(8,128)(2,1)S(1)} %pick_rows.3.refs_0_), channel_id=1, source_target_pairs={{0,64},{64,128},{128,192},{192,0},{1,65},{65,129},{129,193},{193,1... | collective-permute-start | bytes 786440 | tf_op jit(solution)/shard_map/ppermute | solution.py:467
  32.5 22.2 %collective-permute-start.12 = (bf16[512,256]{1,0:T(8,128)(2,1)S(1)}, bf16[512,256]{1,0:T(8,128)(2,1)S(1)}, u32[]{:S(2)}, u32[]{:S(2)}) collective-permute-start(bf16[512,256]{1,0:T(8,128)(2,1)S(1)} %pick_rows.3.refs_0_), channel_id=1, source_target_pairs={{0,128},{64,192},{128,0},{192,64},{1,129},{65,193},{129,1},{193,65... | collective-permute-start | bytes 786440 | tf_op jit(solution)/shard_map/ppermute | solution.py:467
  33.2 1.3 collective-permute-start.9
  33.2 1.5 collective-permute-start.8
  161.0 22.1 %all-to-all-start.7 = ((bf16[16,128,256]{2,1,0:T(8,128)(2,1)}), bf16[16,128,256]{2,1,0:T(8,128)(2,1)S(1)}, u32[]{:S(2)}, u32[]{:S(2)}) async-start(bf16[16,128,256]{2,1,0:T(8,128)(2,1)} %bitcast.3), calls=%async_computation.7 | async-start | bytes 2097152 | tf_op jit(solution)/shard_map/all_to_all | solution.py:484
  165.9 1.9 collective-permute-start.15
  165.9 1.9 collective-permute-start.16
  168.0 11.0 %collective-permute-start.18 = (bf16[144,256]{1,0:T(8,128)(2,1)S(1)}, bf16[144,256]{1,0:T(8,128)(2,1)S(1)}, u32[]{:S(2)}, u32[]{:S(2)}) collective-permute-start(bf16[144,256]{1,0:T(8,128)(2,1)S(1)} %get-tuple-element.68), channel_id=1, source_target_pairs={{0,16},{8,24},{16,32},{24,40},{32,48},{40,56},{48,0},{56,8},{1,17}... | collective-permute-start | bytes 221192 | tf_op jit(solution)/shard_map/ppermute | solution.py:471
  168.5 10.5 %collective-permute-start.19 = (bf16[144,256]{1,0:T(8,128)(2,1)S(1)}, bf16[144,256]{1,0:T(8,128)(2,1)S(1)}, u32[]{:S(2)}, u32[]{:S(2)}) collective-permute-start(bf16[144,256]{1,0:T(8,128)(2,1)S(1)} %get-tuple-element.69), channel_id=1, source_target_pairs={{0,24},{8,32},{16,40},{24,48},{32,56},{40,0},{48,8},{56,16},{1,25}... | collective-permute-start | bytes 221192 | tf_op jit(solution)/shard_map/ppermute | solution.py:471
  169.9 12.3 %collective-permute-start.20 = (bf16[144,256]{1,0:T(8,128)(2,1)S(1)}, bf16[144,256]{1,0:T(8,128)(2,1)S(1)}, u32[]{:S(2)}, u32[]{:S(2)}) collective-permute-start(bf16[144,256]{1,0:T(8,128)(2,1)S(1)} %get-tuple-element.70), channel_id=1, source_target_pairs={{0,32},{8,40},{16,48},{24,56},{32,0},{40,8},{48,16},{56,24},{1,33}... | collective-permute-start | bytes 221192 | tf_op jit(solution)/shard_map/ppermute | solution.py:471
  174.2 8.8 %collective-permute-start.21 = (bf16[144,256]{1,0:T(8,128)(2,1)S(1)}, bf16[144,256]{1,0:T(8,128)(2,1)S(1)}, u32[]{:S(2)}, u32[]{:S(2)}) collective-permute-start(bf16[144,256]{1,0:T(8,128)(2,1)S(1)} %get-tuple-element.71), channel_id=1, source_target_pairs={{0,40},{8,48},{16,56},{24,0},{32,8},{40,16},{48,24},{56,32},{1,41}... | collective-permute-start | bytes 221192 | tf_op jit(solution)/shard_map/ppermute | solution.py:471
  183.9 15.1 %all-to-all-start.8 = ((bf16[4,128,256]{2,1,0:T(8,128)(2,1)}), bf16[4,128,256]{2,1,0:T(8,128)(2,1)S(1)}, u32[]{:S(2)}, u32[]{:S(2)}) async-start(bf16[4,128,256]{2,1,0:T(8,128)(2,1)} %broadcast_in_dim.2), calls=%async_computation.8 | async-start | bytes 524288 | tf_op jit(solution)/shard_map/all_to_all | solution.py:492
  188.8 5.6 %collective-permute-start.17 = (bf16[144,256]{1,0:T(8,128)(2,1)S(1)}, bf16[144,256]{1,0:T(8,128)(2,1)S(1)}, u32[]{:S(2)}, u32[]{:S(2)}) collective-permute-start(bf16[144,256]{1,0:T(8,128)(2,1)S(1)} %get-tuple-element.66), channel_id=1, source_target_pairs={{0,8},{8,16},{16,24},{24,32},{32,40},{40,48},{48,56},{56,0},{1,9},... | collective-permute-start | bytes 221192 | tf_op jit(solution)/shard_map/ppermute | solution.py:471
  191.7 6.2 %collective-permute-start.22 = (bf16[144,256]{1,0:T(8,128)(2,1)S(1)}, bf16[144,256]{1,0:T(8,128)(2,1)S(1)}, u32[]{:S(2)}, u32[]{:S(2)}) collective-permute-start(bf16[144,256]{1,0:T(8,128)(2,1)S(1)} %get-tuple-element.76), channel_id=1, source_target_pairs={{0,48},{8,56},{16,0},{24,8},{32,16},{40,24},{48,32},{56,40},{1,49}... | collective-permute-start | bytes 221192 | tf_op jit(solution)/shard_map/ppermute | solution.py:471
  192.5 5.3 %collective-permute-start.23 = (bf16[144,256]{1,0:T(8,128)(2,1)S(1)}, bf16[144,256]{1,0:T(8,128)(2,1)S(1)}, u32[]{:S(2)}, u32[]{:S(2)}) collective-permute-start(bf16[144,256]{1,0:T(8,128)(2,1)S(1)} %get-tuple-element.77), channel_id=1, source_target_pairs={{0,56},{8,0},{16,8},{24,16},{32,24},{40,32},{48,40},{56,48},{1,57}... | collective-permute-start | bytes 221192 | tf_op jit(solution)/shard_map/ppermute | solution.py:471
where the time goes:
time: 200 us
  blocking collectives  87 us (44%)
  starting transfers between devices  43.3 us (22%)
  Pallas kernels  40.7 us (20%)
  waiting for transfers between devices  22 us (11%)
  local copies, waits for them, and re-layouts  5.91 us (3%)
    all_to_all x4, blocking collectives, over_rows(): return lax.all_to_all(parts, ('x', 'y'), 0, 0, tiled=True)  51.1 us
    all_to_all x3, blocking collectives, over_protos(): return lax.all_to_all(parts, ('z', 'c'), 0, 0, tiled=True)  35.9 us
    ppermute x8, starting transfers between devices, shift_z(): return lax.ppermute(value, 'z', [(i, (i + by) % Z) for i in range(Z)])  18.1 us
    ppermute x8, waiting for transfers between devices, shift_z(): return lax.ppermute(value, 'z', [(i, (i + by) % Z) for i in range(Z)])  13.8 us
    pallas_call x1, Pallas kernels, gradients(): pl.pallas_call(grad_kernel, out_shape=(pltpu.HBM((ROWS, D), BF16), jax.Sh...  13.5 us
    pallas_call x1, Pallas kernels, last_pass(): pl.pallas_call(last_kernel, out_shape=(jax.ShapeDtypeStruct((PEERS, 3 * G...  8.83 us
    ppermute x6, starting transfers between devices, shift_x(): return lax.ppermute(value, 'x', [(i, (i + by) % X) for i in range(X)])  8.62 us
    pallas_call x1, Pallas kernels, teacher_scores(): pl.pallas_call(teacher_kernel, out_shape=(pltpu.VMEM((ROWS, PROTOS), BF16...  6.36 us
  transfers between devices with their start and end apart: 26, of which 10 were waited for; matrix products, arithmetic and copies ran while one was open for 1% of the time, Pallas kernels for 4%

commit v1 on v0

--- a/solution.py
+++ b/solution.py
@@ -106,7 +106,7 @@
     return pl.ds(pl.multiple_of(block * BLOCK, BLOCK), BLOCK)
 
 
-def in_pairs(multiply, work):
+def in_pairs(multiply, work, unroll):
     multiply(0, 0)
 
     def step(pair, carry):
@@ -116,7 +116,7 @@
             work(block, parity)
         return carry
 
-    lax.fori_loop(0, KERN_BLOCKS // 2, step, 0)
+    lax.fori_loop(0, KERN_BLOCKS // 2, step, 0, unroll=unroll)
 
 
 def teacher_kernel(*refs):
@@ -149,7 +149,7 @@
             top_ref[pl.ds(group_at, 1), :] = row
             spread(tops_ref, 0, group_at, row)
 
-    in_pairs(multiply, work)
+    in_pairs(multiply, work, 2)
 
 
 def teacher_scores(rows, protos):
@@ -291,7 +291,7 @@
             spread(sums_ref, GROUPS, group_at, along(crossed) * S_SCALE)
             spread(sums_ref, 2 * GROUPS, group_at, jnp.log2(along(spent)) + top)
 
-    in_pairs(multiply, work)
+    in_pairs(multiply, work, 1)
 
 
 def last_pass(weight, got, protos, rows, kern):
@@ -361,7 +361,7 @@
                 prob = jnp.exp2(scores_refs[parity][at] * (S_SCALE * LOG2E) - lse)
                 logits_refs[parity][at] = (prob - target).astype(BF16)
 
-    in_pairs(multiply, work)
+    in_pairs(multiply, work, 2)
     reduce(KERN_BLOCKS - 1, 1)
 
     core = lax.axis_index("c")
@@ -521,7 +521,7 @@
     for by in (4, 3, 5, 2, 6, 1, 7):
         parts[by] = shift_z(sends[by - 1], by)
     student = over_rows(student.reshape(PEERS, ROWS // PEERS, D))
-    student, parts[2:6] = lax.optimization_barrier((student, parts[2:6]))
+    student, parts[3:6] = lax.optimization_barrier((student, parts[3:6]))
     student = jnp.sum(student.astype(F32), axis=0).astype(BF16)
     student = over_y(jnp.broadcast_to(student[None], (Y,) + student.shape))
     grad_weight, loss = join_sums(mine, parts)

time: 200 us -> 200 us (level)
  transfers between devices with their start and end apart: 26 -> 26, of which waited for: 10 -> 12; matrix products, arithmetic and copies ran while one was open for 1% -> 1% of each run, Pallas kernels for 4% -> 3%
where the time goes in v1:
time: 200 us; the launch traced here: 199 us
  blocking collectives  86.8 us (43%)
  starting transfers between devices  42.2 us (21%)
  Pallas kernels  39.5 us (20%)
  waiting for transfers between devices  23.8 us (12%)
  local copies, waits for them, and re-layouts  5.91 us (3%)
    all_to_all x4, blocking collectives, over_rows(): return lax.all_to_all(parts, ('x', 'y'), 0, 0, tiled=True)  50.9 us
    all_to_all x3, blocking collectives, over_protos(): return lax.all_to_all(parts, ('z', 'c'), 0, 0, tiled=True)  35.9 us
    ppermute x8, starting transfers between devices, shift_z(): return lax.ppermute(value, 'z', [(i, (i + by) % Z) for i in range(Z)])  17.1 us
    ppermute x8, waiting for transfers between devices, shift_z(): return lax.ppermute(value, 'z', [(i, (i + by) % Z) for i in range(Z)])  15.5 us
    pallas_call x1, Pallas kernels, gradients(): pl.pallas_call(grad_kernel, out_shape=(pltpu.HBM((ROWS, D), BF16), jax.Sh...  12.9 us
    pallas_call x1, Pallas kernels, last_pass(): pl.pallas_call(last_kernel, out_shape=(jax.ShapeDtypeStruct((PEERS, 3 * G...  8.82 us
    ppermute x6, starting transfers between devices, shift_x(): return lax.ppermute(value, 'x', [(i, (i + by) % X) for i in range(X)])  8.62 us
    ppermute x3, starting transfers between devices, fan_z(): return lax.ppermute(value, ('z', 'c'), pairs)  5.7 us
  transfers between devices with their start and end apart: 26, of which 12 were waited for; matrix products, arithmetic and copies ran while one was open for 1% of the time, Pallas kernels for 3%

profile of v1, /device:TPU:8, one launch (start us, length us, event | category | flops | bytes accessed | tf_op | source)
XLA Modules:
  0.0 199.1 jit_solution(11208856478259917742)
XLA Ops:
  4.5 4.6 %collective-permute-start.7 = (bf16[256,256]{1,0:T(8,128)(2,1)S(1)}, bf16[256,256]{1,0:T(8,128)(2,1)S(1)}, u32[]{:S(2)}, u32[]{:S(2)}) collective-permute-start(bf16[256,256]{1,0:T(8,128)(2,1)S(1)} %constant_dynamic-update-slice_fusion.refs_4_), channel_id=1, source_target_pairs={{0,24},{4,44},{8,32},{12,52},{16,40},{20,60},{24,48},{28,4},{32,56... | collective-permute-start | bytes 393224 | tf_op jit(solution)/shard_map/ppermute | solution.py:480
  9.1 4.5 %collective-permute-start.6 = (bf16[128,256]{1,0:T(8,128)(2,1)}, bf16[128,256]{1,0:T(8,128)(2,1)S(1)}, u32[]{:S(2)}, u32[]{:S(2)}) collective-permute-start(bf16[128,256]{1,0:T(8,128)(2,1)} %param.7), channel_id=1, source_target_pairs={{0,32},{8,40},{16,48},{24,56},{32,0},{40,8},{48,16},{56,24},{1,33}... | collective-permute-start | bytes 196616 | tf_op jit(solution)/shard_map/ppermute | solution.py:471
  13.6 2.8 %collective-permute-start.2 = (bf16[512,256]{1,0:T(8,128)(2,1)S(1)}, bf16[512,256]{1,0:T(8,128)(2,1)S(1)}, u32[]{:S(2)}, u32[]{:S(2)}) collective-permute-start(bf16[512,256]{1,0:T(8,128)(2,1)S(1)} %pick_rows.2.refs_0_), channel_id=1, source_target_pairs={{0,192},{64,0},{128,64},{192,128},{1,193},{65,1},{129,65},{193,129... | collective-permute-start | bytes 786440 | tf_op jit(solution)/shard_map/ppermute | solution.py:467
  16.3 3.3 %collective-permute-done.6.refs_11_ = bf16[128,256]{1,0:T(8,128)(2,1)S(1)} collective-permute-done((bf16[128,256]{1,0:T(8,128)(2,1)}, bf16[128,256]{1,0:T(8,128)(2,1)S(1)}, u32[]{:S(2)}, u32[]{:S(2)}) %collective-permute-start.6) | collective-permute-done | bytes 65568 | tf_op jit(solution)/shard_map/ppermute | solution.py:471
  19.6 3.0 %collective-permute-start = (bf16[512,256]{1,0:T(8,128)(2,1)S(1)}, bf16[512,256]{1,0:T(8,128)(2,1)S(1)}, u32[]{:S(2)}, u32[]{:S(2)}) collective-permute-start(bf16[512,256]{1,0:T(8,128)(2,1)S(1)} %pick_rows.2.refs_0_), channel_id=1, source_target_pairs={{0,128},{64,192},{128,0},{192,64},{1,129},{65,193},{129,1},{193,65... | collective-permute-start | bytes 786440 | tf_op jit(solution)/shard_map/ppermute | solution.py:467
  23.7 5.1 %collective-permute-done.4.refs_5_ = bf16[256,256]{1,0:T(8,128)(2,1)S(1)} collective-permute-done((bf16[256,256]{1,0:T(8,128)(2,1)S(1)}, bf16[256,256]{1,0:T(8,128)(2,1)S(1)}, u32[]{:S(2)}, u32[]{:S(2)}) %collective-permute-start.4) | collective-permute-done | bytes 131104 | tf_op jit(solution)/shard_map/ppermute | solution.py:480
  34.9 5.6 %teacher_scores.1 = (bf16[2048,2048]{1,0:T(8,128)(2,1)S(1)}, f32[16,128]{1,0:T(8,128)S(1)}, f32[16,16,128]{2,1,0:T(8,128)S(1)}, bf16[2048,256]{1,0:T(8,128)(2,1)S(1)}) custom-call(bf16[512,256]{1,0:T(8,128)(2,1)S(1)} %pick_rows.2.refs_0_, bf16[512,256]{1,0:T(8,128)(2,1)S(1)} %collective-permute-done.refs_1_, ...), custom_call_target="tpu_custom_call" | custom-call | tf_op jit(solution)/shard_map/teacher_scores/pallas_call | solution.py:156
  40.5 13.4 %all_to_all.45.got_ref = f32[16,16,128]{2,1,0:T(8,128)S(1)} all-to-all(f32[16,16,128]{2,1,0:T(8,128)S(1)} %get-tuple-element.46), channel_id=1, replica_groups=mesh['x'=4,'z'=8,'c'=2,'y'=4] {'x','y'}, dimensions={0} | all-to-all | bytes 262144 | tf_op jit(solution)/shard_map/all_to_all | solution.py:484
  53.9 1.8 column_pass.3
  55.8 13.3 %all_to_all.46.got_ref = f32[16,16,128]{2,1,0:T(8,128)S(1)} all-to-all(f32[16,16,128]{2,1,0:T(8,128)S(1)} %column_pass.3), channel_id=1, replica_groups=mesh['x'=4,'z'=8,'c'=2,'y'=4] {'z','c'}, dimensions={0} | all-to-all | bytes 262144 | tf_op jit(solution)/shard_map/all_to_all | solution.py:488
  69.0 2.5 %row_pass.2 = (f32[16,16,128]{2,1,0:T(8,128)S(1)}, f32[16,128]{1,0:T(8,128)}) custom-call(f32[16,128]{1,0:T(8,128)S(1)} %row_weight.1.weight_ref, f32[16,16,128]{2,1,0:T(8,128)S(1)} %all_to_all.46.got_ref, bf16[2048,2048]{1,0:T(8,128)(2,1)S(1)} %get-tuple-element.49.refs_0_.kern_ref.refs_1_.refs_4_), custom_call_target="tpu_custom_call" | custom-call | tf_op jit(solution)/shard_map/row_pass/pallas_call | solution.py:244
  71.5 11.6 %all_to_all.47.refs_0_ = f32[16,16,128]{2,1,0:T(8,128)S(1)} all-to-all(f32[16,16,128]{2,1,0:T(8,128)S(1)} %get-tuple-element.50), channel_id=1, replica_groups=mesh['x'=4,'z'=8,'c'=2,'y'=4] {'x','y'}, dimensions={0} | all-to-all | bytes 262144 | tf_op jit(solution)/shard_map/all_to_all | solution.py:484
  83.2 1.9 column_pass.4
  85.0 11.3 %all_to_all.48.got_ref = f32[16,16,128]{2,1,0:T(8,128)S(1)} all-to-all(f32[16,16,128]{2,1,0:T(8,128)S(1)} %column_pass.4), channel_id=1, replica_groups=mesh['x'=4,'z'=8,'c'=2,'y'=4] {'z','c'}, dimensions={0} | all-to-all | bytes 262144 | tf_op jit(solution)/shard_map/all_to_all | solution.py:488
  96.3 2.5 %row_pass.3 = (f32[16,16,128]{2,1,0:T(8,128)S(1)}, f32[16,128]{1,0:T(8,128)}) custom-call(f32[16,128]{1,0:T(8,128)S(1)} %row_weight.1.weight_ref, f32[16,16,128]{2,1,0:T(8,128)S(1)} %all_to_all.48.got_ref, bf16[2048,2048]{1,0:T(8,128)(2,1)S(1)} %get-tuple-element.49.refs_0_.kern_ref.refs_1_.refs_4_), custom_call_target="tpu_custom_call" | custom-call | tf_op jit(solution)/shard_map/row_pass/pallas_call | solution.py:244
  98.8 11.5 %all_to_all.49.refs_0_ = f32[16,16,128]{2,1,0:T(8,128)S(1)} all-to-all(f32[16,16,128]{2,1,0:T(8,128)S(1)} %get-tuple-element.51), channel_id=1, replica_groups=mesh['x'=4,'z'=8,'c'=2,'y'=4] {'x','y'}, dimensions={0} | all-to-all | bytes 262144 | tf_op jit(solution)/shard_map/all_to_all | solution.py:484
  110.3 1.9 column_pass.5
  112.2 11.3 %all_to_all.50.got_ref = f32[16,16,128]{2,1,0:T(8,128)S(1)} all-to-all(f32[16,16,128]{2,1,0:T(8,128)S(1)} %column_pass.5), channel_id=1, replica_groups=mesh['x'=4,'z'=8,'c'=2,'y'=4] {'z','c'}, dimensions={0} | all-to-all | bytes 262144 | tf_op jit(solution)/shard_map/all_to_all | solution.py:488
  123.5 8.8 %last_pass.1 = (f32[16,48,128]{2,1,0:T(8,128)S(1)}, f32[16,128]{1,0:T(8,128)S(1)}, bf16[2048,256]{1,0:T(8,128)(2,1)S(1)}) custom-call(f32[16,128]{1,0:T(8,128)S(1)} %row_weight.1.weight_ref, f32[16,16,128]{2,1,0:T(8,128)S(1)} %all_to_all.50.got_ref, bf16[2048,256]{1,0:T(8,128)(2,1)S(1)} %get-tuple-element.52.protos_ref, ...), custom_call_target="tpu_custom_call" | custom-call | tf_op jit(solution)/shard_map/last_pass/pallas_call | solution.py:298
  132.3 14.3 %all_to_all.51.got_ref = f32[16,48,128]{2,1,0:T(8,128)S(1)} all-to-all(f32[16,48,128]{2,1,0:T(8,128)S(1)} %get-tuple-element.57), channel_id=1, replica_groups=mesh['x'=4,'z'=8,'c'=2,'y'=4] {'x','y'}, dimensions={0} | all-to-all | bytes 786432 | tf_op jit(solution)/shard_map/all_to_all | solution.py:484
  146.7 12.9 %gradients.1 = (bf16[2048,256]{1,0:T(8,128)(2,1)}, f32[8,128,256]{2,1,0:T(8,128)S(1)}, bf16[8,128,256]{2,1,0:T(8,128)(2,1)S(1)}, f32[8,128]{1,0:T(8,128)S(1)}) custom-call(f32[16,128]{1,0:T(8,128)S(1)} %row_weight.1.weight_ref, f32[16,48,128]{2,1,0:T(8,128)S(1)} %all_to_all.51.got_ref, f32[16,128]{1,0:T(8,128)S(1)} %get-tuple-element.58.scale_ref, ...), custom_call_target="tpu_custom_call" | custom-call | tf_op jit(solution)/shard_map/gradients/pallas_call | solution.py:383
  159.6 4.9 %all-to-all-start.7 = ((bf16[16,128,256]{2,1,0:T(8,128)(2,1)}), bf16[16,128,256]{2,1,0:T(8,128)(2,1)S(1)}, u32[]{:S(2)}, u32[]{:S(2)}) async-start(bf16[16,128,256]{2,1,0:T(8,128)(2,1)} %bitcast.3), calls=%async_computation.7 | async-start | bytes 2097152 | tf_op jit(solution)/shard_map/all_to_all | solution.py:484
  167.4 2.6 %collective-permute-start.20 = (bf16[144,256]{1,0:T(8,128)(2,1)S(1)}, bf16[144,256]{1,0:T(8,128)(2,1)S(1)}, u32[]{:S(2)}, u32[]{:S(2)}) collective-permute-start(bf16[144,256]{1,0:T(8,128)(2,1)S(1)} %get-tuple-element.69), channel_id=1, source_target_pairs={{0,32},{8,40},{16,48},{24,56},{32,0},{40,8},{48,16},{56,24},{1,33}... | collective-permute-start | bytes 221192 | tf_op jit(solution)/shard_map/ppermute | solution.py:471
  170.0 2.6 %collective-permute-start.21 = (bf16[144,256]{1,0:T(8,128)(2,1)S(1)}, bf16[144,256]{1,0:T(8,128)(2,1)S(1)}, u32[]{:S(2)}, u32[]{:S(2)}) collective-permute-start(bf16[144,256]{1,0:T(8,128)(2,1)S(1)} %get-tuple-element.70), channel_id=1, source_target_pairs={{0,40},{8,48},{16,56},{24,0},{32,8},{40,16},{48,24},{56,32},{1,41}... | collective-permute-start | bytes 221192 | tf_op jit(solution)/shard_map/ppermute | solution.py:471
  172.7 3.2 %collective-permute-done.19.refs_3_ = bf16[144,256]{1,0:T(8,128)(2,1)S(1)} collective-permute-done((bf16[144,256]{1,0:T(8,128)(2,1)S(1)}, bf16[144,256]{1,0:T(8,128)(2,1)S(1)}, u32[]{:S(2)}, u32[]{:S(2)}) %collective-permute-start.19) | collective-permute-done | bytes 73760 | tf_op jit(solution)/shard_map/ppermute | solution.py:471
  175.9 2.5 %collective-permute-done.20.refs_4_ = bf16[144,256]{1,0:T(8,128)(2,1)S(1)} collective-permute-done((bf16[144,256]{1,0:T(8,128)(2,1)S(1)}, bf16[144,256]{1,0:T(8,128)(2,1)S(1)}, u32[]{:S(2)}, u32[]{:S(2)}) %collective-permute-start.20) | collective-permute-done | bytes 73760 | tf_op jit(solution)/shard_map/ppermute | solution.py:471
  178.4 2.2 %collective-permute-done.21.refs_5_ = bf16[144,256]{1,0:T(8,128)(2,1)S(1)} collective-permute-done((bf16[144,256]{1,0:T(8,128)(2,1)S(1)}, bf16[144,256]{1,0:T(8,128)(2,1)S(1)}, u32[]{:S(2)}, u32[]{:S(2)}) %collective-permute-start.21) | collective-permute-done | bytes 73760 | tf_op jit(solution)/shard_map/ppermute | solution.py:471
  181.5 4.8 %all-to-all-start.8 = ((bf16[4,128,256]{2,1,0:T(8,128)(2,1)}), bf16[4,128,256]{2,1,0:T(8,128)(2,1)S(1)}, u32[]{:S(2)}, u32[]{:S(2)}) async-start(bf16[4,128,256]{2,1,0:T(8,128)(2,1)} %broadcast_in_dim.2), calls=%async_computation.8 | async-start | bytes 524288 | tf_op jit(solution)/shard_map/all_to_all | solution.py:492
  186.3 2.3 %collective-permute-start.17 = (bf16[144,256]{1,0:T(8,128)(2,1)S(1)}, bf16[144,256]{1,0:T(8,128)(2,1)S(1)}, u32[]{:S(2)}, u32[]{:S(2)}) collective-permute-start(bf16[144,256]{1,0:T(8,128)(2,1)S(1)} %get-tuple-element.65), channel_id=1, source_target_pairs={{0,8},{8,16},{16,24},{24,32},{32,40},{40,48},{48,56},{56,0},{1,9},... | collective-permute-start | bytes 221192 | tf_op jit(solution)/shard_map/ppermute | solution.py:471
  188.6 1.7 collective-permute-start.18
  190.3 2.4 %collective-permute-start.22 = (bf16[144,256]{1,0:T(8,128)(2,1)S(1)}, bf16[144,256]{1,0:T(8,128)(2,1)S(1)}, u32[]{:S(2)}, u32[]{:S(2)}) collective-permute-start(bf16[144,256]{1,0:T(8,128)(2,1)S(1)} %get-tuple-element.74), channel_id=1, source_target_pairs={{0,48},{8,56},{16,0},{24,8},{32,16},{40,24},{48,32},{56,40},{1,49}... | collective-permute-start | bytes 221192 | tf_op jit(solution)/shard_map/ppermute | solution.py:471
  192.8 2.9 %collective-permute-done.18.refs_2_ = bf16[144,256]{1,0:T(8,128)(2,1)S(1)} collective-permute-done((bf16[144,256]{1,0:T(8,128)(2,1)S(1)}, bf16[144,256]{1,0:T(8,128)(2,1)S(1)}, u32[]{:S(2)}, u32[]{:S(2)}) %collective-permute-start.18) | collective-permute-done | bytes 73760 | tf_op jit(solution)/shard_map/ppermute | solution.py:471
  (52 shorter events, 18.1 us)
Async XLA Ops:
  0.6 1.2 copy-start
  1.9 0.7 copy-start.2
  2.9 1.6 collective-permute-start.3
  4.5 18.2 %collective-permute-start.7 = (bf16[256,256]{1,0:T(8,128)(2,1)S(1)}, bf16[256,256]{1,0:T(8,128)(2,1)S(1)}, u32[]{:S(2)}, u32[]{:S(2)}) collective-permute-start(bf16[256,256]{1,0:T(8,128)(2,1)S(1)} %constant_dynamic-update-slice_fusion.refs_4_), channel_id=1, source_target_pairs={{0,24},{4,44},{8,32},{12,52},{16,40},{20,60},{24,48},{28,4},{32,56... | collective-permute-start | bytes 393224 | tf_op jit(solution)/shard_map/ppermute | solution.py:480
  9.1 10.5 %collective-permute-start.6 = (bf16[128,256]{1,0:T(8,128)(2,1)}, bf16[128,256]{1,0:T(8,128)(2,1)S(1)}, u32[]{:S(2)}, u32[]{:S(2)}) collective-permute-start(bf16[128,256]{1,0:T(8,128)(2,1)} %param.7), channel_id=1, source_target_pairs={{0,32},{8,40},{16,48},{24,56},{32,0},{40,8},{48,16},{56,24},{1,33}... | collective-permute-start | bytes 196616 | tf_op jit(solution)/shard_map/ppermute | solution.py:471
  13.6 18.1 %collective-permute-start.2 = (bf16[512,256]{1,0:T(8,128)(2,1)S(1)}, bf16[512,256]{1,0:T(8,128)(2,1)S(1)}, u32[]{:S(2)}, u32[]{:S(2)}) collective-permute-start(bf16[512,256]{1,0:T(8,128)(2,1)S(1)} %pick_rows.2.refs_0_), channel_id=1, source_target_pairs={{0,192},{64,0},{128,64},{192,128},{1,193},{65,1},{129,65},{193,129... | collective-permute-start | bytes 786440 | tf_op jit(solution)/shard_map/ppermute | solution.py:467
  16.3 16.2 %collective-permute-start.1 = (bf16[512,256]{1,0:T(8,128)(2,1)S(1)}, bf16[512,256]{1,0:T(8,128)(2,1)S(1)}, u32[]{:S(2)}, u32[]{:S(2)}) collective-permute-start(bf16[512,256]{1,0:T(8,128)(2,1)S(1)} %pick_rows.2.refs_0_), channel_id=1, source_target_pairs={{0,64},{64,128},{128,192},{192,0},{1,65},{65,129},{129,193},{193,1... | collective-permute-start | bytes 786440 | tf_op jit(solution)/shard_map/ppermute | solution.py:467
  16.3 7.4 %collective-permute-start.5 = (bf16[256,256]{1,0:T(8,128)(2,1)S(1)}, bf16[256,256]{1,0:T(8,128)(2,1)S(1)}, u32[]{:S(2)}, u32[]{:S(2)}) collective-permute-start(bf16[256,256]{1,0:T(8,128)(2,1)S(1)} %constant_dynamic-update-slice_fusion.refs_4_), channel_id=1, source_target_pairs={{0,16},{4,52},{8,24},{12,60},{16,32},{20,4},{24,40},{28,12},{32,48... | collective-permute-start | bytes 393224 | tf_op jit(solution)/shard_map/ppermute | solution.py:480
  19.6 13.6 %collective-permute-start = (bf16[512,256]{1,0:T(8,128)(2,1)S(1)}, bf16[512,256]{1,0:T(8,128)(2,1)S(1)}, u32[]{:S(2)}, u32[]{:S(2)}) collective-permute-start(bf16[512,256]{1,0:T(8,128)(2,1)S(1)} %pick_rows.2.refs_0_), channel_id=1, source_target_pairs={{0,128},{64,192},{128,0},{192,64},{1,129},{65,193},{129,1},{193,65... | collective-permute-start | bytes 786440 | tf_op jit(solution)/shard_map/ppermute | solution.py:467
  22.6 6.2 %collective-permute-start.4 = (bf16[256,256]{1,0:T(8,128)(2,1)S(1)}, bf16[256,256]{1,0:T(8,128)(2,1)S(1)}, u32[]{:S(2)}, u32[]{:S(2)}) collective-permute-start(bf16[256,256]{1,0:T(8,128)(2,1)S(1)} %constant_dynamic-update-slice_fusion.refs_4_), channel_id=1, source_target_pairs={{0,8},{4,60},{8,16},{12,4},{16,24},{20,12},{24,32},{28,20},{32,40}... | collective-permute-start | bytes 393224 | tf_op jit(solution)/shard_map/ppermute | solution.py:480
  23.7 9.5 %collective-permute-start.10 = (bf16[256,256]{1,0:T(8,128)(2,1)S(1)}, bf16[256,256]{1,0:T(8,128)(2,1)S(1)}, u32[]{:S(2)}, u32[]{:S(2)}) collective-permute-start(bf16[256,256]{1,0:T(8,128)(2,1)S(1)} %collective-permute-done.7.refs_7_), channel_id=1, source_target_pairs={{0,4},{4,0},{1,5},{5,1},{2,6},{6,2},{3,7},{7,3},{8,12},{12,8},{9,1... | collective-permute-start | bytes 393224 | tf_op jit(solution)/shard_map/ppermute | solution.py:475
  28.8 1.6 collective-permute-start.11
  28.8 1.2 copy-start.1
  30.4 23.5 %collective-permute-start.14 = (bf16[512,256]{1,0:T(8,128)(2,1)S(1)}, bf16[512,256]{1,0:T(8,128)(2,1)S(1)}, u32[]{:S(2)}, u32[]{:S(2)}) collective-permute-start(bf16[512,256]{1,0:T(8,128)(2,1)S(1)} %pick_rows.3.refs_0_), channel_id=1, source_target_pairs={{0,192},{64,0},{128,64},{192,128},{1,193},{65,1},{129,65},{193,129... | collective-permute-start | bytes 786440 | tf_op jit(solution)/shard_map/ppermute | solution.py:467
  31.6 22.3 %collective-permute-start.13 = (bf16[512,256]{1,0:T(8,128)(2,1)S(1)}, bf16[512,256]{1,0:T(8,128)(2,1)S(1)}, u32[]{:S(2)}, u32[]{:S(2)}) collective-permute-start(bf16[512,256]{1,0:T(8,128)(2,1)S(1)} %pick_rows.3.refs_0_), channel_id=1, source_target_pairs={{0,64},{64,128},{128,192},{192,0},{1,65},{65,129},{129,193},{193,1... | collective-permute-start | bytes 786440 | tf_op jit(solution)/shard_map/ppermute | solution.py:467
  32.5 21.4 %collective-permute-start.12 = (bf16[512,256]{1,0:T(8,128)(2,1)S(1)}, bf16[512,256]{1,0:T(8,128)(2,1)S(1)}, u32[]{:S(2)}, u32[]{:S(2)}) collective-permute-start(bf16[512,256]{1,0:T(8,128)(2,1)S(1)} %pick_rows.3.refs_0_), channel_id=1, source_target_pairs={{0,128},{64,192},{128,0},{192,64},{1,129},{65,193},{129,1},{193,65... | collective-permute-start | bytes 786440 | tf_op jit(solution)/shard_map/ppermute | solution.py:467
  33.2 1.3 collective-permute-start.9
  33.2 1.6 collective-permute-start.8
  159.6 21.0 %all-to-all-start.7 = ((bf16[16,128,256]{2,1,0:T(8,128)(2,1)}), bf16[16,128,256]{2,1,0:T(8,128)(2,1)S(1)}, u32[]{:S(2)}, u32[]{:S(2)}) async-start(bf16[16,128,256]{2,1,0:T(8,128)(2,1)} %bitcast.3), calls=%async_computation.7 | async-start | bytes 2097152 | tf_op jit(solution)/shard_map/all_to_all | solution.py:484
  164.5 1.9 collective-permute-start.15
  164.5 1.9 collective-permute-start.16
  166.6 9.3 %collective-permute-start.19 = (bf16[144,256]{1,0:T(8,128)(2,1)S(1)}, bf16[144,256]{1,0:T(8,128)(2,1)S(1)}, u32[]{:S(2)}, u32[]{:S(2)}) collective-permute-start(bf16[144,256]{1,0:T(8,128)(2,1)S(1)} %get-tuple-element.68), channel_id=1, source_target_pairs={{0,24},{8,32},{16,40},{24,48},{32,56},{40,0},{48,8},{56,16},{1,25}... | collective-permute-start | bytes 221192 | tf_op jit(solution)/shard_map/ppermute | solution.py:471
  167.4 10.9 %collective-permute-start.20 = (bf16[144,256]{1,0:T(8,128)(2,1)S(1)}, bf16[144,256]{1,0:T(8,128)(2,1)S(1)}, u32[]{:S(2)}, u32[]{:S(2)}) collective-permute-start(bf16[144,256]{1,0:T(8,128)(2,1)S(1)} %get-tuple-element.69), channel_id=1, source_target_pairs={{0,32},{8,40},{16,48},{24,56},{32,0},{40,8},{48,16},{56,24},{1,33}... | collective-permute-start | bytes 221192 | tf_op jit(solution)/shard_map/ppermute | solution.py:471
  170.0 10.6 %collective-permute-start.21 = (bf16[144,256]{1,0:T(8,128)(2,1)S(1)}, bf16[144,256]{1,0:T(8,128)(2,1)S(1)}, u32[]{:S(2)}, u32[]{:S(2)}) collective-permute-start(bf16[144,256]{1,0:T(8,128)(2,1)S(1)} %get-tuple-element.70), channel_id=1, source_target_pairs={{0,40},{8,48},{16,56},{24,0},{32,8},{40,16},{48,24},{56,32},{1,41}... | collective-permute-start | bytes 221192 | tf_op jit(solution)/shard_map/ppermute | solution.py:471
  181.5 16.9 %all-to-all-start.8 = ((bf16[4,128,256]{2,1,0:T(8,128)(2,1)}), bf16[4,128,256]{2,1,0:T(8,128)(2,1)S(1)}, u32[]{:S(2)}, u32[]{:S(2)}) async-start(bf16[4,128,256]{2,1,0:T(8,128)(2,1)} %broadcast_in_dim.2), calls=%async_computation.8 | async-start | bytes 524288 | tf_op jit(solution)/shard_map/all_to_all | solution.py:492
  186.3 6.5 %collective-permute-start.17 = (bf16[144,256]{1,0:T(8,128)(2,1)S(1)}, bf16[144,256]{1,0:T(8,128)(2,1)S(1)}, u32[]{:S(2)}, u32[]{:S(2)}) collective-permute-start(bf16[144,256]{1,0:T(8,128)(2,1)S(1)} %get-tuple-element.65), channel_id=1, source_target_pairs={{0,8},{8,16},{16,24},{24,32},{32,40},{40,48},{48,56},{56,0},{1,9},... | collective-permute-start | bytes 221192 | tf_op jit(solution)/shard_map/ppermute | solution.py:471
  188.6 7.1 %collective-permute-start.18 = (bf16[144,256]{1,0:T(8,128)(2,1)S(1)}, bf16[144,256]{1,0:T(8,128)(2,1)S(1)}, u32[]{:S(2)}, u32[]{:S(2)}) collective-permute-start(bf16[144,256]{1,0:T(8,128)(2,1)S(1)} %get-tuple-element.66), channel_id=1, source_target_pairs={{0,16},{8,24},{16,32},{24,40},{32,48},{40,56},{48,0},{56,8},{1,17}... | collective-permute-start | bytes 221192 | tf_op jit(solution)/shard_map/ppermute | solution.py:471
  190.3 6.0 %collective-permute-start.22 = (bf16[144,256]{1,0:T(8,128)(2,1)S(1)}, bf16[144,256]{1,0:T(8,128)(2,1)S(1)}, u32[]{:S(2)}, u32[]{:S(2)}) collective-permute-start(bf16[144,256]{1,0:T(8,128)(2,1)S(1)} %get-tuple-element.74), channel_id=1, source_target_pairs={{0,48},{8,56},{16,0},{24,8},{32,16},{40,24},{48,32},{56,40},{1,49}... | collective-permute-start | bytes 221192 | tf_op jit(solution)/shard_map/ppermute | solution.py:471
  192.7 4.4 %collective-permute-start.23 = (bf16[144,256]{1,0:T(8,128)(2,1)S(1)}, bf16[144,256]{1,0:T(8,128)(2,1)S(1)}, u32[]{:S(2)}, u32[]{:S(2)}) collective-permute-start(bf16[144,256]{1,0:T(8,128)(2,1)S(1)} %get-tuple-element.75), channel_id=1, source_target_pairs={{0,56},{8,0},{16,8},{24,16},{32,24},{40,32},{48,40},{56,48},{1,57}... | collective-permute-start | bytes 221192 | tf_op jit(solution)/shard_map/ppermute | solution.py:471
